TPU v7x, 128 devices: a whole 4x4x4 slice. The times are simulated.
128 devices in a mesh: row: 16 (over y_lo, x, core), col: 8 (over z, y_hi).
Axes of the slice: x: 4, y: 4 (y_hi: 2, y_lo: 2; y = y_hi * 2 + y_lo), z: 4, core: 2. Of those that a mesh axis runs over, the one named last changes fastest.
Arguments:
- features: bfloat16 [65536, 128], P(('row', 'col')), may hold values from -6 to 6
- degree: int32 [65536], P(('row', 'col')), may hold values from 32 to 512
- cotangent: bfloat16 [65536, 256], P(('row', 'col')), may hold values from -24 to 24
- weight: bfloat16 [128, 256], replicated, may hold values from -0.5 to 0.5
- layer_bias: float32 [256], replicated, may hold values from -3 to 3
- patterns: bfloat16 [64, 128, 128], replicated, may hold values from 0 to 1, as said below
- tile_row: int32 [16, 8, 512], P('row', 'col'), may hold values from 0 to 31
- tile_col: int32 [16, 8, 512], P('row', 'col'), may hold values from 0 to 63
- tile_pattern: int32 [16, 8, 512], P('row', 'col'), may hold values from 0 to 63
- tile_weight: int32 [16, 8, 512], P('row', 'col'), may hold values from 1 to 4
- tile_count: int32 [16, 8], P('row', 'col'), may hold values from 64 to 512, as said below
Outputs:
- activations: bfloat16 [65536, 256], P(('row', 'col'))
- grad_features: bfloat16 [65536, 128], P(('row', 'col'))
- grad_weight: float32 [128, 256], replicated
- grad_bias: float32 [256], replicated
Inputs may be any that keep to these rules, and one draw needn't show every extreme that they name: `tile_row`: slots may name the same tile position more than once; such tiles add. `tile_count`: 512 is reached at some grid position in every draw. `patterns`: entries are 0 or 1.
All inputs are finite; a program needn't handle non-finite values.
Results may differ from a plain program's by a relative error of at most 0.0058.
Values may be sent and summed in bfloat16 or wider, within the bound.
No kernel may reach another device: no remote copies, remote signals or barrier semaphores. Data moves between devices by JAX's collectives and lax.ppermute only.
A program may use at most 128 MiB of HBM per device.

v0:
```python
import math

import jax
import jax.numpy as jnp
from jax import lax
from jax.sharding import PartitionSpec as P


def gelu_slope(values, upstream):
    return jax.vjp(lambda inner: jax.nn.gelu(inner, approximate=True), values)[1](upstream)[0]


def aggregate(
    panel, sources, targets, pattern_ids, multiples, live_count, patterns, target_count, transposed
):
    tile_edge = patterns.shape[1]
    hidden = panel.shape[1]
    panel_tiles = panel.reshape(panel.shape[0] // tile_edge, tile_edge, hidden)
    group_size = min(32, sources.shape[0])
    turn_count = (live_count + group_size - 1) // group_size
    einsum_form = "kba,kbh->kah" if transposed else "kab,kbh->kah"

    def one_turn(turn_index, totals):
        start_slot = turn_index * group_size
        source_ids = lax.dynamic_slice_in_dim(sources, start_slot, group_size)
        target_ids = lax.dynamic_slice_in_dim(targets, start_slot, group_size)
        chosen_ids = lax.dynamic_slice_in_dim(pattern_ids, start_slot, group_size)
        chosen_weights = lax.dynamic_slice_in_dim(multiples, start_slot, group_size)
        live_mask = start_slot + jnp.arange(group_size, dtype=jnp.int32) < live_count
        factor = jnp.where(live_mask, chosen_weights, 0).astype(jnp.bfloat16)
        matrices = patterns[chosen_ids] * factor[:, None, None]
        blocks = panel_tiles[source_ids]
        products = jnp.einsum(einsum_form, matrices, blocks, preferred_element_type=jnp.float32)
        return totals.at[target_ids].add(products)

    initial = jnp.zeros((target_count, tile_edge, hidden), jnp.float32)
    totals = lax.fori_loop(jnp.int32(0), turn_count, one_turn, initial)
    return totals.reshape(target_count * tile_edge, hidden)


def per_device(
    features,
    degree,
    cotangent,
    weight,
    layer_bias,
    patterns,
    tile_row,
    tile_col,
    tile_pattern,
    tile_weight,
    tile_count,
):
    node_dev = features.shape[0]
    row_devices = lax.axis_size("row")
    col_devices = lax.axis_size("col")
    tile_edge = patterns.shape[1]
    live_count = tile_count[0, 0]
    rows_local = tile_row[0, 0]
    cols_local = tile_col[0, 0]
    pattern_local = tile_pattern[0, 0]
    weight_local = tile_weight[0, 0]
    inv_root = lax.rsqrt(degree.astype(jnp.float32))
    scaled = (
        inv_root[:, None] * jnp.dot(features, weight, preferred_element_type=jnp.float32)
    ).astype(jnp.bfloat16)
    col_panel = lax.all_gather(scaled, "row", axis=0, tiled=True)
    row_partial = aggregate(
        col_panel,
        cols_local,
        rows_local,
        pattern_local,
        weight_local,
        live_count,
        patterns,
        col_devices * node_dev // tile_edge,
        False,
    )
    row_total = lax.psum(row_partial, "col")
    cotangent_block, degree_block = (
        lax.all_gather(cotangent, "col", axis=0, tiled=True),
        lax.all_gather(degree, "col", axis=0, tiled=True),
    )
    inv_block = lax.rsqrt(degree_block.astype(jnp.float32))
    pre_block = inv_block[:, None] * row_total + layer_bias[None, :]
    own_start = lax.axis_index("col") * node_dev
    own_pre = lax.dynamic_slice_in_dim(pre_block, own_start, node_dev, 0)
    activations = jax.nn.gelu(own_pre, approximate=True).astype(jnp.bfloat16)
    slope_block = gelu_slope(pre_block, cotangent_block.astype(jnp.float32))
    row_panel = (inv_block[:, None] * slope_block).astype(jnp.bfloat16)
    own_slope = lax.dynamic_slice_in_dim(slope_block, own_start, node_dev, 0)
    col_partial = aggregate(
        row_panel,
        rows_local,
        cols_local,
        pattern_local,
        weight_local,
        live_count,
        patterns,
        row_devices * node_dev // tile_edge,
        True,
    )
    col_share = lax.psum_scatter(col_partial, "row", scatter_dimension=0, tiled=True)
    grad_hidden = (inv_root[:, None] * col_share).astype(jnp.bfloat16)
    grad_features = lax.dot_general(
        grad_hidden, weight, (((1,), (1,)), ((), ())), preferred_element_type=jnp.float32
    ).astype(jnp.bfloat16)
    weight_term = lax.dot_general(
        features, grad_hidden, (((0,), (0,)), ((), ())), preferred_element_type=jnp.float32
    )
    bias_term = jnp.sum(own_slope, axis=0)
    weight_total, bias_total = lax.psum((weight_term, bias_term), ("row", "col"))
    scale_factor = 1.0 / math.sqrt(node_dev * row_devices * col_devices)
    return (activations, grad_features, weight_total * scale_factor, bias_total * scale_factor)


def solution(mesh):
    in_specs = (
        P(("row", "col"), None),
        P(("row", "col")),
        P(("row", "col"), None),
        P(),
        P(),
        P(),
        P("row", "col", None),
        P("row", "col", None),
        P("row", "col", None),
        P("row", "col", None),
        P("row", "col"),
    )
    out_specs = (P(("row", "col"), None), P(("row", "col"), None), P(), P())
    return jax.shard_map(
        per_device, mesh=mesh, in_specs=in_specs, out_specs=out_specs, check_vma=False
    )
```

profile of v0, /device:TPU:1, one launch (start us, length us, event | category | flops | bytes accessed | tf_op | source)
XLA Modules:
  0.0 1066.5 jit_solution(9198207579307350021)
XLA Ops:
  11.3 40.0 %all-gather.4.cloned.1.call-done = bf16[8192,256]{1,0:T(8,128)(2,1)} async-done(((bf16[512,256]{1,0:T(8,128)(2,1)}), bf16[8192,256]{1,0:T(8,128)(2,1)}) %all-gather.4.cloned.1.call-update) | async-done | bytes 4194320 | tf_op jit(solution)/shard_map/all_gather | solution.py:67
  51.3 2.5 broadcast_in_dim.34
  53.8 56.4 %while.20 = (s32[]{:T(128)}, f32[32,128,256]{2,1,0:T(8,128)}, s32[]{:T(128)}, s32[512]{0:T(512)S(1)}, s32[512]{0:T(512)S(1)}, /*index=5*/bf16[64,128,128]{2,1,0:...) while((s32[]{:T(128)}, f32[32,128,256]{2,1,0:T(8,128)}, ...), condition=%wide.region_2.3_spmd, body=%wide.region_0.2_spmd.sunk | while | flops 270010784 | bytes 26224452 | solution.py:37
  54.6 2.3 gather_fusion.1
  57.0 2.9 gather_fusion
  59.8 2.7 fusion.41
  62.6 10.1 scatter_fusion
  73.5 2.4 gather_fusion.1
  75.8 2.9 gather_fusion
  78.7 2.7 fusion.41
  81.5 10.1 scatter_fusion
  92.3 2.4 gather_fusion.1
  94.7 2.9 gather_fusion
  97.6 2.7 fusion.41
  100.3 9.9 scatter_fusion
  110.9 117.9 %all-gather = s32[8,1,512]{2,1,0:T(1,128)S(1)} all-gather(s32[1,1,512]{2,1,0:T(1,128)S(1)} %bitcast.36), channel_id=1, replica_groups=mesh['row'=16,'col'=8] {'col'}, dimensions={0}, use_global_device_ids=true | all-gather | bytes 18432 | tf_op jit(solution)/shard_map/all_gather | solution.py:82
  228.9 305.5 %all-reduce.3.cloned.1.call-done = f32[4096,256]{1,0:T(8,128)} async-done(((f32[4096,256]{1,0:T(8,128)}), f32[4096,256]{1,0:T(8,128)}) %all-reduce.3.cloned.1.call-update) | async-done | bytes 4194320 | tf_op jit(solution)/shard_map/psum | solution.py:79
  534.3 7.7 multiply_convert_fusion
  542.0 4.3 broadcast_in_dim.35
  546.3 55.4 %while.21 = (s32[]{:T(128)}, f32[64,128,256]{2,1,0:T(8,128)}, s32[]{:T(128)}, s32[512]{0:T(512)S(1)}, s32[512]{0:T(512)S(1)}, /*index=5*/bf16[64,128,128]{2,1,0:...) while((s32[]{:T(128)}, f32[64,128,256]{2,1,0:T(8,128)}, ...), condition=%wide.region_6.7_spmd, body=%wide.region_4.6_spmd.sunk | while | flops 270010784 | bytes 26224452 | solution.py:37
  547.1 2.3 gather_fusion.3
  551.7 3.1 fusion.44
  554.8 10.0 scatter_fusion.1
  565.6 2.3 gather_fusion.3
  570.2 3.1 fusion.44
  573.3 9.9 scatter_fusion.1
  584.0 2.3 gather_fusion.3
  586.4 2.3 gather_fusion.2
  588.6 3.1 fusion.44
  591.7 10.0 scatter_fusion.1
  602.9 307.8 %psum.23 = f32[256]{0:T(256)S(1)} all-reduce(f32[256]{0:T(256)S(1)} %dynamic-slice_reduce_fusion), channel_id=1, replica_groups=mesh['row'=16,'col'=8] {'row','col'}, use_global_device_ids=true, to_apply=%region_10.11 | all-reduce | flops 256 | bytes 2048 | tf_op jit(solution)/shard_map/psum | solution.py:112
  917.3 141.0 %all-reduce.5.cloned.1.call-done = f32[128,256]{0,1:T(8,128)} async-done(((f32[128,256]{0,1:T(8,128)}), f32[128,256]{0,1:T(8,128)}) %all-reduce.5.cloned.1.call-update) | async-done | bytes 131088 | tf_op jit(solution)/shard_map/psum | solution.py:112
  (64 shorter events, 22.9 us)
Async XLA Ops:
  7.2 0.9 copy-start
  7.2 46.6 %copy-start.4 = (s32[1,1,512]{2,1,0:T(1,128)S(1)}, s32[1,1,512]{2,1,0:T(1,128)}, u32[]{:S(2)}) copy-start(s32[1,1,512]{2,1,0:T(1,128)} %param.24) | copy-start | bytes 6148
  7.2 46.6 %copy-start.3 = (s32[1,1,512]{2,1,0:T(1,128)S(1)}, s32[1,1,512]{2,1,0:T(1,128)}, u32[]{:S(2)}) copy-start(s32[1,1,512]{2,1,0:T(1,128)} %param.23) | copy-start | bytes 6148
  7.2 46.6 %copy-start.5 = (s32[1,1,512]{2,1,0:T(1,128)S(1)}, s32[1,1,512]{2,1,0:T(1,128)}, u32[]{:S(2)}) copy-start(s32[1,1,512]{2,1,0:T(1,128)} %param.22) | copy-start | bytes 6148
  7.2 46.6 %copy-start.2 = (s32[1,1,512]{2,1,0:T(1,128)S(1)}, s32[1,1,512]{2,1,0:T(1,128)}, u32[]{:S(2)}) copy-start(s32[1,1,512]{2,1,0:T(1,128)} %param.21) | copy-start | bytes 6148
  7.2 44.1 %all-gather.4.cloned.1.call-start = ((), (), s32[]{:S(2)}) async-start(), calls=%async_computation.1 | async-start | bytes 4456448 | tf_op jit(solution)/shard_map/all_gather | solution.py:67
  9.9 219.0 %all-gather.6.cloned.1.call-start = ((), (), s32[]{:S(2)}) async-start(), calls=%async_computation.3 | async-start | bytes 2359296 | tf_op jit(solution)/shard_map/all_gather | solution.py:81
  10.6 523.7 %all-reduce.3.cloned.1.call-start = ((), (), s32[]{:S(2)}) async-start(), calls=%async_computation.2 | async-start | bytes 8388608 | tf_op jit(solution)/shard_map/psum | solution.py:79
  110.2 0.7 copy-start.6
  110.2 424.1 %copy-start.7 = (f32[256]{0:T(256)S(1)}, f32[256]{0:T(256)}, u32[]{:S(2)}) copy-start(f32[256]{0:T(256)} %param.19) | copy-start | bytes 3076
  110.2 803.0 %reduce-scatter.2.cloned.1.call-start = ((), (), s32[]{:S(2)}) async-start(), calls=%async_computation.4 | async-start | bytes 8912896 | tf_op jit(solution)/shard_map/reduce_scatter | solution.py:103
  601.7 313.6 %copy-start.1 = (bf16[128,256]{1,0:T(8,128)(2,1)S(1)}, bf16[128,256]{1,0:T(8,128)(2,1)}, u32[]{:S(2)}) copy-start(bf16[128,256]{1,0:T(8,128)(2,1)} %param.18) | copy-start | bytes 196612
  601.8 456.6 %all-reduce.5.cloned.1.call-start = ((), (), s32[]{:S(2)}) async-start(), calls=%async_computation.5 | async-start | bytes 262144 | tf_op jit(solution)/shard_map/psum | solution.py:112
Sparse Core Ops, SparseCore 0:
  10.3 40.9 all-gather.3
  53.6 53.4 all-gather.5
  110.4 423.9 all-reduce.2
  601.9 308.7 reduce-scatter.1
  915.9 142.3 all-reduce.4
where the time goes:
time: 1070 us
  waiting for transfers between devices  487 us (46%)
  blocking collectives  426 us (40%)
  other arithmetic  77.7 us (7%)
  local copies, waits for them, and re-layouts  37.7 us (4%)
  matrix products  23.2 us (2%)
  between operations  14.5 us (1%)
    psum x1, blocking collectives, per_device(): lax.psum((weight_term, bias_term), ('row', 'col'))  308 us
    psum x1, waiting for transfers between devices, per_device(): row_total = lax.psum(row_partial, 'col')  305 us
    psum x1, waiting for transfers between devices, per_device(): lax.psum((weight_term, bias_term), ('row', 'col'))  141 us
    all_gather x1, blocking collectives, per_device(): lax.all_gather(degree, 'col', axis=0, tiled=True)  118 us
    scatter-add x6, other arithmetic, one_turn(): return totals.at[target_ids].add(products)  59.9 us
    all_gather x1, waiting for transfers between devices, per_device(): col_panel = lax.all_gather(scaled, 'row', axis=0, tiled=True)  40 us
  transfers between devices with their start and end apart: 5, of which 3 were waited for; matrix products, arithmetic and copies ran while one was open for 6% of the time, Pallas kernels for 0%

commit v1 on v0

v1 whole, which is shorter than its diff:
```python
import math

import jax
import jax.numpy as jnp
from jax import lax
from jax.experimental import pallas as pl
from jax.experimental.pallas import tpu as pltpu
from jax.sharding import PartitionSpec as P

GROUP = 8
VMEM_LIMIT = 48 * 1024 * 1024
ROOT_2_PI = math.sqrt(2.0 / math.pi)
CUBIC = 0.044715


def tile_sums_kernel(
    count_ref, source_ref, target_ref, pattern_ref, multiple_ref, patterns_ref, panel_ref, out_ref
):
    edge = patterns_ref.shape[1]
    live = count_ref[0, 0]
    out_ref[...] = jnp.zeros_like(out_ref)

    def one_group(group, carry):
        terms = []
        for member in range(GROUP):
            slot = group * GROUP + member
            factor = jnp.where(slot < live, multiple_ref[slot], 0).astype(jnp.float32)
            tile = patterns_ref[pattern_ref[slot]]
            start = pl.multiple_of(source_ref[slot] * edge, edge)
            block = panel_ref[pl.ds(start, edge), :]
            product = jnp.dot(tile, block, preferred_element_type=jnp.float32)
            terms.append((target_ref[slot], factor, product))
        for target, factor, product in terms:
            rows = pl.ds(pl.multiple_of(target * edge, edge), edge)
            out_ref[rows, :] += factor * product
        return carry

    lax.fori_loop(0, (live + GROUP - 1) // GROUP, one_group, 0)


def tile_sums(count, sources, targets, pattern_ids, multiples, patterns, panel, target_count):
    smem = pl.BlockSpec(memory_space=pltpu.SMEM)
    vmem = pl.BlockSpec(memory_space=pltpu.VMEM)
    edge = patterns.shape[1]
    width = panel.shape[1]
    slots = sources.shape[0]
    return pl.pallas_call(
        tile_sums_kernel,
        out_shape=jax.ShapeDtypeStruct((target_count * edge, width), jnp.float32),
        in_specs=[smem] * 5 + [vmem] * 2,
        out_specs=vmem,
        compiler_params=pltpu.CompilerParams(vmem_limit_bytes=VMEM_LIMIT),
        cost_estimate=pl.CostEstimate(
            flops=2 * slots * edge * edge * width,
            bytes_accessed=patterns.size * 2 + panel.size * 2 + target_count * edge * width * 4,
            transcendentals=0,
        ),
    )(count, sources, targets, pattern_ids, multiples, patterns, panel)


def split_product(left, right, dims):
    high = left.astype(jnp.bfloat16)
    low = (left - high.astype(jnp.float32)).astype(jnp.bfloat16)
    return lax.dot_general(
        high, right, (dims, ((), ())), preferred_element_type=jnp.float32
    ) + lax.dot_general(low, right, (dims, ((), ())), preferred_element_type=jnp.float32)


def middle_kernel(
    sums_ref, degree_ref, cotangent_ref, weight_ref, bias_ref, act_ref, spread_ref, grads_ref
):
    inv_root = lax.rsqrt(degree_ref[...].astype(jnp.float32))
    sums = sums_ref[...]
    weight = weight_ref[...]
    pre_act = inv_root * split_product(sums, weight, ((1,), (0,))) + bias_ref[...]
    square = pre_act * pre_act
    bent = jnp.tanh(ROOT_2_PI * (pre_act + CUBIC * (pre_act * square)))
    half = 0.5 * (1.0 + bent)
    act_ref[...] = (pre_act * half).astype(jnp.bfloat16)
    rise = 0.5 * pre_act * (1.0 - bent * bent) * (ROOT_2_PI * (1.0 + 3.0 * CUBIC * square))
    slope = cotangent_ref[...].astype(jnp.float32) * (half + rise)
    upstream = (inv_root * slope).astype(jnp.bfloat16)
    spread_ref[...] = lax.dot_general(
        upstream, weight, (((1,), (1,)), ((), ())), preferred_element_type=jnp.float32
    ).astype(jnp.bfloat16)
    feature_count = weight.shape[0]
    grads_ref[:feature_count, :] = split_product(sums, upstream, ((0,), (0,)))
    bias_row = jnp.sum(slope, axis=0, keepdims=True)
    row_ids = lax.broadcasted_iota(jnp.int32, (8, bias_row.shape[1]), 0)
    grads_ref[feature_count:, :] = jnp.where(row_ids == 0, bias_row, 0.0)


def middle(sums, degree, cotangent, weight, bias):
    vmem = pl.BlockSpec(memory_space=pltpu.VMEM)
    nodes, hidden = cotangent.shape
    feature_count = weight.shape[0]
    return pl.pallas_call(
        middle_kernel,
        out_shape=(
            jax.ShapeDtypeStruct((nodes, hidden), jnp.bfloat16),
            jax.ShapeDtypeStruct((nodes, feature_count), jnp.bfloat16),
            jax.ShapeDtypeStruct((feature_count + 8, hidden), jnp.float32),
        ),
        in_specs=[vmem] * 5,
        out_specs=(vmem,) * 3,
        compiler_params=pltpu.CompilerParams(vmem_limit_bytes=VMEM_LIMIT),
    )(sums, degree[:, None], cotangent, weight, bias[None, :])


def per_device(
    features,
    degree,
    cotangent,
    weight,
    layer_bias,
    patterns,
    tile_row,
    tile_col,
    tile_pattern,
    tile_weight,
    tile_count,
):
    node_dev = features.shape[0]
    row_devices = lax.axis_size("row")
    col_devices = lax.axis_size("col")
    tile_edge = patterns.shape[1]
    rows_local = tile_row[0, 0]
    cols_local = tile_col[0, 0]
    pattern_local = tile_pattern[0, 0]
    weight_local = tile_weight[0, 0]
    turned = jnp.swapaxes(patterns, 1, 2)
    inv_root = lax.rsqrt(degree.astype(jnp.float32))

    scaled = (inv_root[:, None] * features.astype(jnp.float32)).astype(jnp.bfloat16)
    col_panel = lax.all_gather(scaled, "row", axis=0, tiled=True)
    row_partial = tile_sums(
        tile_count,
        cols_local,
        rows_local,
        pattern_local,
        weight_local,
        patterns,
        col_panel,
        col_devices * node_dev // tile_edge,
    )
    own_sums = lax.psum_scatter(row_partial, "col", scatter_dimension=0, tiled=True)
    activations, spread, grads = middle(own_sums, degree, cotangent, weight, layer_bias)
    grads_total = lax.psum(grads, ("row", "col"))
    row_panel = lax.all_gather(spread, "col", axis=0, tiled=True)
    col_partial = tile_sums(
        tile_count,
        rows_local,
        cols_local,
        pattern_local,
        weight_local,
        turned,
        row_panel,
        row_devices * node_dev // tile_edge,
    )
    own_back = lax.psum_scatter(col_partial, "row", scatter_dimension=0, tiled=True)
    grad_features = (inv_root[:, None] * own_back).astype(jnp.bfloat16)
    scale_factor = 1.0 / math.sqrt(node_dev * row_devices * col_devices)
    feature_count = weight.shape[0]
    return (
        activations,
        grad_features,
        grads_total[:feature_count] * scale_factor,
        grads_total[feature_count] * scale_factor,
    )


def solution(mesh):
    in_specs = (
        P(("row", "col"), None),
        P(("row", "col")),
        P(("row", "col"), None),
        P(),
        P(),
        P(),
        P("row", "col", None),
        P("row", "col", None),
        P("row", "col", None),
        P("row", "col", None),
        P("row", "col"),
    )
    out_specs = (P(("row", "col"), None), P(("row", "col"), None), P(), P())
    return jax.shard_map(
        per_device, mesh=mesh, in_specs=in_specs, out_specs=out_specs, check_vma=False
    )
```

time: 1070 us -> 409 us (0.38)
  blocking collectives: 426 us -> 0 us
  waiting for transfers between devices: 487 us -> 356 us
  other arithmetic: 77.7 us -> 6.95 us
  local copies, waits for them, and re-layouts: 37.7 us -> 12.5 us
  matrix products: 23.2 us -> 0 us
  Pallas kernels: 0 us -> 15.5 us
    psum x2 -> x1, waiting for transfers between devices: 446 us -> 134 us  [per_device(): grads_total = lax.psum(grads, ('row', 'col'))]
    psum x1 -> x0, blocking collectives: 308 us -> none  [per_device(): lax.psum((weight_term, bias_term), ('row', 'col'))]
    all_gather x1 -> x0, blocking collectives: 118 us -> none  [per_device(): lax.all_gather(degree, 'col', axis=0, tiled=True)]
    reduce_scatter x0 -> x1, waiting for transfers between devices: none -> 81 us  [per_device(): lax.psum_scatter(row_partial, 'col', scatter_dimension=0, tiled=True)]
    reduce_scatter x1, waiting for transfers between devices: 0.01 us -> 60.4 us  [per_device(): lax.psum_scatter(col_partial, 'row', scatter_dimension=0, tiled=True)]
    scatter-add x6 -> x0, other arithmetic: 59.9 us -> none  [one_turn(): return totals.at[target_ids].add(products)]
    all_gather x1, waiting for transfers between devices: 0.02 us -> 42.6 us  [per_device(): row_panel = lax.all_gather(spread, 'col', axis=0, tiled=True)]
    gather x12 -> x0, local copies, waits for them, and re-layouts: 29.5 us -> none  [the longest x6 15.4 us: one_turn(): blocks = panel_tiles[source_ids]]
  transfers between devices with their start and end apart: 5 -> 5, of which waited for: 3 -> 5; matrix products, arithmetic and copies ran while one was open for 6% -> 1% of each run, Pallas kernels for 0% -> 2%
where the time goes in v1:
time: 409 us; the launch traced here: 406 us
  waiting for transfers between devices  356 us (87%)
  Pallas kernels  15.5 us (4%)
  between operations  14.5 us (4%)
  local copies, waits for them, and re-layouts  12.5 us (3%)
  other arithmetic  6.95 us (2%)
    psum x1, waiting for transfers between devices, per_device(): grads_total = lax.psum(grads, ('row', 'col'))  134 us
    reduce_scatter x1, waiting for transfers between devices, per_device(): lax.psum_scatter(row_partial, 'col', scatter_dimension=0, tiled=True)  81 us
    reduce_scatter x1, waiting for transfers between devices, per_device(): lax.psum_scatter(col_partial, 'row', scatter_dimension=0, tiled=True)  60.4 us
    all_gather x1, waiting for transfers between devices, per_device(): row_panel = lax.all_gather(spread, 'col', axis=0, tiled=True)  42.6 us
    all_gather x1, waiting for transfers between devices, per_device(): col_panel = lax.all_gather(scaled, 'row', axis=0, tiled=True)  37.6 us
    pallas_call x2, Pallas kernels, tile_sums(): pl.pallas_call(tile_sums_kernel, out_shape=jax.ShapeDtypeStruct((target_c...  13.9 us
    unnamed x37, local copies, waits for them, and re-layouts  12.3 us
  transfers between devices with their start and end apart: 5, of which 5 were waited for; matrix products, arithmetic and copies ran while one was open for 1% of the time, Pallas kernels for 2%

profile of v1, /device:TPU:1, one launch (start us, length us, event | category | flops | bytes accessed | tf_op | source)
XLA Modules:
  0.0 405.7 jit_solution(10003630610427038370)
XLA Ops:
  7.2 0.0 all-gather.3.cloned.1.call-start
  7.2 0.7 convert_rsqrt_fusion
  7.9 1.7 multiply_convert_fusion.1
  9.6 0.0 all-gather.3.cloned.1.call-update
  9.6 0.0 reduce-scatter.3.cloned.1.call-start
  10.3 37.6 %all-gather.3.cloned.1.call-done.panel_ref = bf16[8192,128]{1,0:T(8,128)(2,1)} async-done(((bf16[512,128]{1,0:T(8,128)(2,1)}), bf16[8192,128]{1,0:T(8,128)(2,1)}) %all-gather.3.cloned.1.call-update) | async-done | bytes 2097168 | tf_op jit(solution)/shard_map/all_gather | solution.py:135
  47.9 1.6 copy-done
  49.5 0.7 copy-done.9
  50.2 0.7 copy-done.11
  50.9 0.7 copy-done.13
  51.5 0.7 copy-done.15
  52.2 6.4 %shard_map.138 = f32[4096,128]{1,0:T(8,128)S(1)} custom-call(s32[1,1]{1,0:T(1,128)S(6)} %copy.19.count_ref, s32[512]{0:T(512)S(1)} %bitcast.10, s32[512]{0:T(512)S(1)} %bitcast.12, s32[512]{0:T(512)S(1)} %bitcast.14, s32[512]{0:T(512)S(1)} %bitcast.16, bf16[64,128,128]{2,1,0:T(8,128)(2,1)S(1)} %copy-done, ...), custom_call_target="tpu_custom_call" | custom-call | flops 2147483648 | bytes 6291456 | tf_op jit(solution)/shard_map/pallas_call | solution.py:47
  58.6 1.3 copy-done.3
  60.0 0.0 reduce-scatter.3.cloned.1.call-update
  60.0 0.0 all-gather.5.cloned.1.call-start
  60.1 0.1 copy.16.degree_ref
  60.2 81.0 %reduce-scatter.3.cloned.1.call-done.sums_ref = f32[512,128]{1,0:T(8,128)} async-done(((f32[4096,128]{1,0:T(8,128)}), f32[512,128]{1,0:T(8,128)}) %reduce-scatter.3.cloned.1.call-update) | async-done | bytes 262160 | tf_op jit(solution)/shard_map/reduce_scatter | solution.py:146
  141.2 0.9 copy-done.5
  142.2 1.6 shard_map.139
  143.8 0.0 all-gather.5.cloned.1.call-update
  143.9 0.0 all-reduce.2.cloned.1.call-start
  143.9 2.9 copy.17
  146.8 0.0 reduce-scatter.5.cloned.1.call-start
  146.9 42.6 %all-gather.5.cloned.1.call-done.panel_ref = bf16[4096,128]{1,0:T(8,128)(2,1)} async-done(((bf16[512,128]{1,0:T(8,128)(2,1)}), bf16[4096,128]{1,0:T(8,128)(2,1)}) %all-gather.5.cloned.1.call-update) | async-done | bytes 1048592 | tf_op jit(solution)/shard_map/all_gather | solution.py:149
  189.5 1.6 copy-done.2
  191.1 1.2 copy-done.8
  192.3 7.5 %shard_map.140 = f32[8192,128]{1,0:T(8,128)} custom-call(s32[1,1]{1,0:T(1,128)S(6)} %copy.19.count_ref, s32[512]{0:T(512)S(1)} %bitcast.13, s32[512]{0:T(512)S(1)} %bitcast.11, s32[512]{0:T(512)S(1)} %bitcast.15, s32[512]{0:T(512)S(1)} %bitcast.17, bf16[64,128,128]{2,1,0:T(8,128)(2,1)S(1)} %bitcast.8, bf16[4096,128]{1,0:T(8,128)(2,1)S(1)} %copy-done.8), custom_call_target="tpu_custom_call" | custom-call | flops 2147483648 | bytes 7340032 | tf_op jit(solution)/shard_map/pallas_call | solution.py:47
  199.8 134.3 %all-reduce.2.cloned.1.call-done = f32[136,256]{1,0:T(8,128)} async-done(((f32[136,256]{1,0:T(8,128)}), f32[136,256]{1,0:T(8,128)}) %all-reduce.2.cloned.1.call-update) | async-done | bytes 139280 | tf_op jit(solution)/shard_map/psum | solution.py:148
  334.1 1.3 slice_multiply_fusion.1
  335.4 1.6 slice_multiply_fusion
  337.0 60.4 %reduce-scatter.5.cloned.1.call-done = f32[512,128]{1,0:T(8,128)} async-done(((f32[8192,128]{1,0:T(8,128)}), f32[512,128]{1,0:T(8,128)}) %reduce-scatter.5.cloned.1.call-update) | async-done | bytes 262160 | tf_op jit(solution)/shard_map/reduce_scatter | solution.py:160
  397.4 1.7 multiply_convert_fusion
  (29 shorter events, 0.1 us)
Async XLA Ops:
  7.2 40.7 %all-gather.3.cloned.1.call-start = ((), (), s32[]{:S(2)}) async-start(), calls=%async_computation.2 | async-start | bytes 2228224 | tf_op jit(solution)/shard_map/all_gather | solution.py:135
  9.6 131.6 %reduce-scatter.3.cloned.1.call-start = ((), (), s32[]{:S(2)}) async-start(), calls=%async_computation.3 | async-start | bytes 2359296 | tf_op jit(solution)/shard_map/reduce_scatter | solution.py:146
  47.9 1.6 copy-start
  49.5 0.7 copy-start.9
  50.2 0.7 copy-start.11
  50.9 0.7 copy-start.13
  51.5 0.7 copy-start.15
  52.2 7.8 %copy-start.17 = (s32[512]{0:T(512)S(1)}, s32[512]{0:T(512)}, u32[]{:S(2)}) copy-start(s32[512]{0:T(512)} %param.12) | copy-start | bytes 6148
  52.2 89.0 %copy-start.6 = (bf16[128,256]{1,0:T(8,128)(2,1)S(1)}, bf16[128,256]{1,0:T(8,128)(2,1)}, u32[]{:S(2)}) copy-start(bf16[128,256]{1,0:T(8,128)(2,1)} %weight_ref.1) | copy-start | bytes 196612
  58.6 1.3 copy-start.3
  60.0 81.2 %copy-start.4 = (bf16[512,256]{1,0:T(8,128)(2,1)S(1)}, bf16[512,256]{1,0:T(8,128)(2,1)}, u32[]{:S(2)}) copy-start(bf16[512,256]{1,0:T(8,128)(2,1)} %cotangent_ref.1) | copy-start | bytes 786436
  60.0 81.2 %copy-start.7 = (f32[256]{0:T(256)S(1)}, f32[256]{0:T(256)}, u32[]{:S(2)}) copy-start(f32[256]{0:T(256)} %param.15) | copy-start | bytes 3076
  60.0 83.9 %copy-start.1 = (bf16[64,128,128]{2,1,0:T(8,128)(2,1)S(1)}, bf16[64,128,128]{2,1,0:T(8,128)(2,1)}, u32[]{:S(2)}) copy-start(bf16[64,128,128]{2,1,0:T(8,128)(2,1)} %patterns_ref.1) | copy-start | bytes 6291460
  60.0 129.5 %all-gather.5.cloned.1.call-start = ((), (), s32[]{:S(2)}) async-start(), calls=%async_computation.4 | async-start | bytes 1179648 | tf_op jit(solution)/shard_map/all_gather | solution.py:149
  141.2 1.0 copy-start.5
  143.8 45.7 %copy-start.10 = (s32[1,1,512]{2,1,0:T(1,128)S(1)}, s32[1,1,512]{2,1,0:T(1,128)}, u32[]{:S(2)}) copy-start(s32[1,1,512]{2,1,0:T(1,128)} %param.18) | copy-start | bytes 6148
  143.8 45.7 %copy-start.12 = (s32[1,1,512]{2,1,0:T(1,128)S(1)}, s32[1,1,512]{2,1,0:T(1,128)}, u32[]{:S(2)}) copy-start(s32[1,1,512]{2,1,0:T(1,128)} %param.17) | copy-start | bytes 6148
  143.8 45.7 %copy-start.14 = (s32[1,1,512]{2,1,0:T(1,128)S(1)}, s32[1,1,512]{2,1,0:T(1,128)}, u32[]{:S(2)}) copy-start(s32[1,1,512]{2,1,0:T(1,128)} %param.19) | copy-start | bytes 6148
  143.8 45.6 %copy-start.16 = (s32[1,1,512]{2,1,0:T(1,128)S(1)}, s32[1,1,512]{2,1,0:T(1,128)}, u32[]{:S(2)}) copy-start(s32[1,1,512]{2,1,0:T(1,128)} %param.20) | copy-start | bytes 6148
  143.9 190.3 %all-reduce.2.cloned.1.call-start = ((), (), s32[]{:S(2)}) async-start(), calls=%async_computation.6 | async-start | bytes 278528 | tf_op jit(solution)/shard_map/psum | solution.py:148
  146.8 250.6 %reduce-scatter.5.cloned.1.call-start = ((), (), s32[]{:S(2)}) async-start(), calls=%async_computation.5 | async-start | bytes 4456448 | tf_op jit(solution)/shard_map/reduce_scatter | solution.py:160
  189.5 1.6 copy-start.2
  191.1 1.2 copy-start.8
Sparse Core Ops, SparseCore 0:
  10.3 37.5 all-gather.2
  60.1 81.0 reduce-scatter.2
  144.1 45.2 all-gather.4
  194.1 140.0 all-reduce.1
  336.5 60.8 reduce-scatter.4
